TPU v7x, 256 devices: a whole 4x4x8 slice. The times are simulated.
256 devices in a mesh: dp: 32 (over z, x), tensor: 8 (over y, core).
Axes of the slice: x: 4, y: 4, z: 8, core: 2. Of those that a mesh axis runs over, the one named last changes fastest.
Arguments:
- activations: bfloat16 [28672, 4096], P('dp', 'tensor'), may hold values from -6 to 6
- out_grads: bfloat16 [28672, 4096], P('dp', 'tensor'), may hold values from -6 to 6
- gate_act: bfloat16 [28672, 14336], P('dp', 'tensor'), may hold values from -6 to 6
- w_down: bfloat16 [14336, 4096], P('tensor', 'dp'), may hold values from -0.09375 to 0.09375
- proj_in: bfloat16 [4096, 64], P('tensor'), may hold values from -0.09375 to 0.09375
- proj_out: bfloat16 [14336, 64], P('tensor'), may hold values from -0.046875 to 0.046875
- lengths: int32 [32, 8], P('dp'), may hold values from 1 to 448, 896 in all within a row
- assign: int32 [256], replicated, may hold values from 0 to 255, each once
Outputs:
- loggrads: float32 [256, 64, 64], P('dp', 'tensor')
Inputs may be any that keep to these rules, and one draw needn't show every extreme that they name: `lengths`: each row gives the token counts of the 8 sequences packed into one data group's 896 rows and sums to 896. `assign`: a permutation of the sequence numbers.
All inputs are finite; a program needn't handle non-finite values.
Results may differ from a plain program's by a relative error of at most 0.013.
Values may be sent and summed in bfloat16 or wider, within the bound.
No kernel may reach another device: no remote copies, remote signals or barrier semaphores. Data moves between devices by JAX's collectives and lax.ppermute only.
A program may use at most 128 MiB of HBM per device.

v0:
```python
import jax
import jax.numpy as jnp
from jax import lax
from jax.sharding import PartitionSpec as P


def shards(activations, out_grads, gate_act, w_down, proj_in, proj_out, lengths, assign):
    tok_rows = activations.shape[0]
    rank_all = proj_in.shape[1]
    full_grads = lax.all_gather(out_grads, "tensor", axis=1, tiled=True)
    hidden_grad = lax.dot_general(
        full_grads,
        lax.all_gather(w_down, "dp", axis=1, tiled=True),
        (((1,), (1,)), ((), ())),
        preferred_element_type=jnp.float32,
    )
    up_grad = (hidden_grad * gate_act.astype(jnp.float32)).astype(jnp.bfloat16)
    out_part = jnp.dot(up_grad, proj_out, preferred_element_type=jnp.float32)
    in_part = jnp.dot(activations, proj_in, preferred_element_type=jnp.float32)
    col_count = rank_all // lax.axis_size("tensor")
    shard_index = lax.axis_index("tensor")
    in_sum, out_sum = lax.psum((in_part, out_part), "tensor")
    in_mine = lax.dynamic_slice_in_dim(in_sum, shard_index * col_count, col_count, 1)
    seq_lengths = lengths[0]
    seq_ends = jnp.cumsum(seq_lengths)
    starts = seq_ends - seq_lengths
    positions = lax.iota(jnp.int32, tok_rows)
    inside = (positions[None, :] >= starts[:, None]) & (positions[None, :] < seq_ends[:, None])
    member = jnp.where(inside, 1.0 / seq_lengths[:, None].astype(jnp.float32), 0.0)
    weighted = member[:, :, None] * in_mine[None, :, :]
    result = jnp.einsum("ctp,tq->cpq", weighted, out_sum, precision=lax.Precision.HIGHEST)
    per_group = seq_lengths.shape[0]
    group_count = lax.axis_size("dp")
    seq_total = per_group * group_count
    group_index = lax.axis_index("dp")
    mine_ids = lax.dynamic_slice_in_dim(assign, group_index * per_group, per_group, 0)
    placing = (mine_ids[None, :] == lax.iota(jnp.int32, seq_total)[:, None]).astype(jnp.float32)
    flat_result = result.reshape(per_group, col_count * rank_all)
    spread = jnp.dot(placing, flat_result, precision=lax.Precision.HIGHEST)
    owned = lax.psum_scatter(
        spread.astype(jnp.bfloat16), "dp", scatter_dimension=0, tiled=True
    ).astype(jnp.float32)
    return owned.reshape(per_group, col_count, rank_all)


def solution(mesh):
    in_specs = (
        P("dp", "tensor"),
        P("dp", "tensor"),
        P("dp", "tensor"),
        P("tensor", "dp"),
        P("tensor", None),
        P("tensor", None),
        P("dp", None),
        P(),
    )
    out_specs = P("dp", "tensor", None)
    return jax.shard_map(shards, mesh=mesh, in_specs=in_specs, out_specs=out_specs, check_vma=False)
```

profile of v0, /device:TPU:8, one launch (start us, length us, event | category | flops | bytes accessed | tf_op | source)
XLA Modules:
  0.0 511.5 jit_solution(17634856475808253684)
XLA Ops:
  6.5 0.0 copy-start
  6.5 0.0 all-gather.3.cloned.1.call-start
  6.5 0.7 all-gather.3.cloned.1.call-update
  7.3 0.0 all-gather.5.cloned.1.call-start
  7.3 0.7 all-gather.5.cloned.1.call-update
  8.0 0.0 all-reduce.3.cloned.1.call-start
  8.1 0.8 reduce-window.7
  8.9 0.7 bitcast_subtract_fusion
  9.5 0.0 copy-done
  9.5 2.0 fusion.10
  11.5 0.0 copy-start.2
  11.5 0.0 copy-start.1
  11.5 47.6 %all-gather.3.cloned.1.call-done = bf16[896,4096]{1,0:T(8,128)(2,1)} async-done(((bf16[896,512]{1,0:T(8,128)(2,1)}), bf16[896,4096]{1,0:T(8,128)(2,1)}) %all-gather.3.cloned.1.call-update) | async-done | bytes 7340048 | tf_op jit(solution)/shard_map/all_gather | solution.py:10
  59.1 142.3 %all-gather.5.cloned.1.call-done = bf16[1792,4096]{1,0:T(8,128)(2,1)} async-done(((bf16[1792,128]{1,0:T(8,128)(2,1)}), bf16[1792,4096]{1,0:T(8,128)(2,1)}) %all-gather.5.cloned.1.call-update) | async-done | bytes 14680080 | tf_op jit(solution)/shard_map/all_gather | solution.py:13
  201.4 23.2 %fusion = f32[896,64]{0,1:T(8,128)} fusion(bf16[1792,64]{0,1:T(8,128)(2,1)} %param.13, bf16[896,1792]{1,0:T(8,128)(2,1)} %param.10, bf16[896,4096]{1,0:T(8,128)(2,1)} %all-gather.3.cloned.1.call-done, bf16[1792,4096]{1,0:T(8,128)(2,1)} %all-gather.5.cloned.1.call-done), kind=kOutput, calls=%fused_computation.1 | convolution fusion | flops 13363675136 | bytes 25690112 | tf_op jit(solution)/shard_map/dot_general | solution.py:18
  224.6 0.0 all-reduce.3.cloned.1.call-update
  224.7 0.0 reduce-scatter.2.cloned.1.call-start
  224.7 0.0 copy-done.2
  224.7 0.0 copy-done.1
  224.8 0.1 dynamic_slice.6
  224.8 0.1 fusion.8
  224.9 60.4 %all-reduce.3.cloned.1.call-done = (f32[896,64]{0,1:T(8,128)}, f32[896,64]{0,1:T(8,128)}) async-done(((f32[896,64]{0,1:T(8,128)}, f32[896,64]{0,1:T(8,128)}), (f32[896,64]{0,1:T(8,128)}, f32[896,64]{0,1:T(8,128)})) %all-reduce.3.cloned.1.call-update) | async-done | bytes 458768 | tf_op jit(solution)/shard_map/psum | solution.py:22
  285.3 0.8 constant_dynamic-slice_fusion
  286.1 1.3 fusion.1
  287.4 0.1 reshape.108
  287.5 1.0 convolution_convert_fusion
  288.5 0.0 reduce-scatter.2.cloned.1.call-update
  288.5 215.0 %reduce-scatter.2.cloned.1.call-done = bf16[8,512]{1,0:T(8,128)(2,1)} async-done(((bf16[256,512]{1,0:T(8,128)(2,1)}), bf16[8,512]{1,0:T(8,128)(2,1)}) %reduce-scatter.2.cloned.1.call-update) | async-done | bytes 8208 | tf_op jit(solution)/shard_map/reduce_scatter | solution.py:40
  503.6 1.4 reshape.112
  (1 shorter events, 0.0 us)
Async XLA Ops:
  6.5 3.0 copy-start
  6.5 52.6 %all-gather.3.cloned.1.call-start = ((), (), s32[]{:S(2)}) async-start(), calls=%async_computation.1 | async-start | bytes 8257536 | tf_op jit(solution)/shard_map/all_gather | solution.py:10
  7.3 194.2 %all-gather.5.cloned.1.call-start = ((), (), s32[]{:S(2)}) async-start(), calls=%async_computation.2 | async-start | bytes 15138816 | tf_op jit(solution)/shard_map/all_gather | solution.py:13
  8.0 277.3 %all-reduce.3.cloned.1.call-start = ((), (), s32[]{:S(2)}) async-start(), calls=%async_computation.4 | async-start | bytes 917504 | tf_op jit(solution)/shard_map/psum | solution.py:22
  11.5 213.2 %copy-start.2 = (s32[1,8]{1,0:T(1,128)S(1)}, s32[1,8]{1,0:T(1,128)}, u32[]{:S(2)}) copy-start(s32[1,8]{1,0:T(1,128)} %param.14) | copy-start | bytes 100
  11.5 213.2 %copy-start.1 = (s32[256]{0:T(256)S(1)}, s32[256]{0:T(256)}, u32[]{:S(2)}) copy-start(s32[256]{0:T(256)} %param.15) | copy-start | bytes 3076
  224.7 278.9 %reduce-scatter.2.cloned.1.call-start = ((), (), s32[]{:S(2)}) async-start(), calls=%async_computation.3 | async-start | bytes 270336 | tf_op jit(solution)/shard_map/reduce_scatter | solution.py:40
Sparse Core Ops, SparseCore 0:
  9.2 49.8 all-gather.2
  61.6 139.7 all-gather.4
  224.8 60.4 all-reduce.2
  289.5 214.0 reduce-scatter.1
where the time goes:
time: 512 us; the launch traced here: 511 us
  waiting for transfers between devices  467 us (91%)
  matrix products  27.5 us (5%)
  between operations  13.2 us (3%)
    reduce_scatter x1, waiting for transfers between devices, shards(): lax.psum_scatter(spread.astype(jnp.bfloat16), 'dp', scatter_dimension=0,...  215 us
    all_gather x1, waiting for transfers between devices, shards(): lax.all_gather(w_down, 'dp', axis=1, tiled=True)  142 us
    psum x1, waiting for transfers between devices, shards(): in_sum, out_sum = lax.psum((in_part, out_part), 'tensor')  60.4 us
    all_gather x1, waiting for transfers between devices, shards(): full_grads = lax.all_gather(out_grads, 'tensor', axis=1, tiled=True)  47.6 us
    dot_general x1, matrix products, shards(): out_part = jnp.dot(up_grad, proj_out, preferred_element_type=jnp.float32)  23.2 us
  transfers between devices with their start and end apart: 4, of which 4 were waited for; matrix products, arithmetic and copies ran while one was open for 1% of the time, Pallas kernels for 0%

commit v1 on v0

--- a/solution.py
+++ b/solution.py
@@ -4,10 +4,28 @@
 from jax.sharding import PartitionSpec as P
 
 
+def laid_out(blocks, dim):
+    dims = list(blocks.shape[1:])
+    dims[dim] *= blocks.shape[0]
+    return jnp.moveaxis(blocks, 0, dim).reshape(dims)
+
+
 def shards(activations, out_grads, gate_act, w_down, proj_in, proj_out, lengths, assign):
     tok_rows = activations.shape[0]
     rank_all = proj_in.shape[1]
-    full_grads = lax.all_gather(out_grads, "tensor", axis=1, tiled=True)
+    size = lax.axis_size("tensor")
+    pairs = [(i, (i + 1) % size) for i in range(size)]
+    back = [(b, a) for a, b in pairs]
+    lower, upper = ([], [])
+    for step in range(size - 1):
+        if step % 2 == 0:
+            lower.append(lax.ppermute(lower[-1] if lower else out_grads, "tensor", pairs))
+        else:
+            upper.append(lax.ppermute(upper[-1] if upper else out_grads, "tensor", back))
+    blocks = jnp.stack([*lower[::-1], out_grads, *upper])
+    shift = lax.axis_index("tensor") - len(lower)
+    blocks = blocks[(jnp.arange(size) - shift) % size]
+    full_grads = laid_out(blocks, 1)
     hidden_grad = lax.dot_general(
         full_grads,
         lax.all_gather(w_down, "dp", axis=1, tiled=True),

time: 512 us -> 462 us (0.902)
  waiting for transfers between devices: 467 us -> 378 us
  local copies, waits for them, and re-layouts: 2.3 us -> 36 us
  starting transfers between devices: 0.12 us -> 5.33 us
    all_gather x1, waiting for transfers between devices: 142 us -> 58.4 us  [shards(): lax.all_gather(w_down, 'dp', axis=1, tiled=True)]
    all_gather x1 -> x0, waiting for transfers between devices: 47.6 us -> none  [shards(): full_grads = lax.all_gather(out_grads, 'tensor', axis=1, tiled=True)]
    ppermute x0 -> x7, waiting for transfers between devices: none -> 43.2 us  [the longest x4 43.2 us: shards(): lax.ppermute(lower[-1] if lower else out_grads, 'tensor', pairs)]
    unnamed x6 -> x19, local copies, waits for them, and re-layouts: 0.01 us -> 13.9 us
    transpose x0 -> x1, local copies, waits for them, and re-layouts: none -> 11.6 us  [laid_out(): return jnp.moveaxis(blocks, 0, dim).reshape(dims)]
    gather x0 -> x1, local copies, waits for them, and re-layouts: none -> 7.2 us  [shards(): blocks = blocks[(jnp.arange(size) - shift) % size]]
    ppermute x0 -> x7, starting transfers between devices: none -> 5.25 us  [the longest x3 5.23 us: shards(): lax.ppermute(upper[-1] if upper else out_grads, 'tensor', back)]
  transfers between devices with their start and end apart: 4 -> 10, of which waited for: 4 -> 7; matrix products, arithmetic and copies ran while one was open for 1% -> 8% of each run, Pallas kernels for 0% -> 0%
where the time goes in v1:
time: 462 us; the launch traced here: 461 us
  waiting for transfers between devices  378 us (82%)
  local copies, waits for them, and re-layouts  36 us (8%)
  matrix products  27.1 us (6%)
  between operations  13.2 us (3%)
  starting transfers between devices  5.33 us (1%)
    reduce_scatter x1, waiting for transfers between devices, shards(): lax.psum_scatter(spread.astype(jnp.bfloat16), 'dp', scatter_dimension=0,...  215 us
    psum x1, waiting for transfers between devices, shards(): in_sum, out_sum = lax.psum((in_part, out_part), 'tensor')  60.4 us
    all_gather x1, waiting for transfers between devices, shards(): lax.all_gather(w_down, 'dp', axis=1, tiled=True)  58.4 us
    ppermute x4, waiting for transfers between devices, shards(): lax.ppermute(lower[-1] if lower else out_grads, 'tensor', pairs)  43.2 us
    dot_general x1, matrix products, shards(): out_part = jnp.dot(up_grad, proj_out, preferred_element_type=jnp.float32)  22.7 us
    unnamed x19, local copies, waits for them, and re-layouts  13.9 us
    transpose x1, local copies, waits for them, and re-layouts, laid_out(): return jnp.moveaxis(blocks, 0, dim).reshape(dims)  11.6 us
  transfers between devices with their start and end apart: 10, of which 7 were waited for; matrix products, arithmetic and copies ran while one was open for 8% of the time, Pallas kernels for 0%

profile of v1, /device:TPU:8, one launch (start us, length us, event | category | flops | bytes accessed | tf_op | source)
XLA Modules:
  0.0 461.0 jit_solution(18018525603241624923)
XLA Ops:
  6.5 0.0 copy-start
  6.5 0.0 copy-start.1
  6.5 0.0 all-gather.2.cloned.1.call-start
  6.5 0.7 all-gather.2.cloned.1.call-update
  7.3 0.0 all-reduce.3.cloned.1.call-start
  7.3 0.0 collective-permute-start
  7.3 13.0 %collective-permute-done = bf16[896,512]{1,0:T(8,128)(2,1)S(1)} collective-permute-done((bf16[896,512]{1,0:T(8,128)(2,1)}, bf16[896,512]{1,0:T(8,128)(2,1)S(1)}, u32[]{:S(2)}, u32[]{:S(2)}) %collective-permute-start) | collective-permute-done | bytes 917536 | tf_op jit(solution)/shard_map/ppermute | solution.py:22
  20.3 0.0 collective-permute-start.1
  20.4 1.7 collective-permute-start.4
  22.1 11.1 %collective-permute-done.1 = bf16[896,512]{1,0:T(8,128)(2,1)S(1)} collective-permute-done((bf16[896,512]{1,0:T(8,128)(2,1)S(1)}, bf16[896,512]{1,0:T(8,128)(2,1)S(1)}, u32[]{:S(2)}, u32[]{:S(2)}) %collective-permute-start.1) | collective-permute-done | bytes 917536 | tf_op jit(solution)/shard_map/ppermute | solution.py:22
  33.2 0.0 copy-start.2
  33.2 0.9 copy-done.2
  34.1 0.0 collective-permute-start.2
  34.1 0.0 collective-permute-done.4
  34.1 1.7 collective-permute-start.5
  35.8 11.2 %collective-permute-done.2 = bf16[896,512]{1,0:T(8,128)(2,1)} collective-permute-done((bf16[896,512]{1,0:T(8,128)(2,1)S(1)}, bf16[896,512]{1,0:T(8,128)(2,1)}, u32[]{:S(2)}, u32[]{:S(2)}) %collective-permute-start.2) | collective-permute-done | bytes 917536 | tf_op jit(solution)/shard_map/ppermute | solution.py:22
  47.0 0.0 collective-permute-start.3
  47.0 0.8 reduce-window.7
  47.9 0.7 bitcast_subtract_fusion
  48.5 0.0 copy-done
  48.5 2.0 fusion.12
  50.5 0.0 collective-permute-done.5
  50.5 1.7 collective-permute-start.6
  52.2 7.9 %collective-permute-done.3 = bf16[896,512]{1,0:T(8,128)(2,1)} collective-permute-done((bf16[896,512]{1,0:T(8,128)(2,1)}, bf16[896,512]{1,0:T(8,128)(2,1)}, u32[]{:S(2)}, u32[]{:S(2)}) %collective-permute-start.3) | collective-permute-done | bytes 917536 | tf_op jit(solution)/shard_map/ppermute | solution.py:22
  60.2 2.2 bitcast_dynamic-update-slice_fusion.7
  62.3 2.2 bitcast_dynamic-update-slice_fusion.6
  64.5 2.2 bitcast_dynamic-update-slice_fusion.5
  66.7 1.0 bitcast_dynamic-update-slice_fusion.4
  67.7 0.0 copy-done.1
  67.7 1.0 bitcast_dynamic-update-slice_fusion.3
  68.7 2.2 bitcast_dynamic-update-slice_fusion.2
  70.9 2.2 bitcast_dynamic-update-slice_fusion.1
  73.1 0.0 collective-permute-done.6
  73.1 1.0 bitcast_dynamic-update-slice_fusion
  74.1 7.2 %gather_fusion = bf16[8,896,512]{2,1,0:T(8,128)(2,1)} fusion(bf16[8,896,512]{2,1,0:T(8,128)(2,1)} %bitcast_dynamic-update-slice_fusion, s32[1024]{0:T(1024)S(1)} %pad_clamp_fusion), kind=kCustom, calls=%fused_computation | custom fusion | bytes 14680096 | tf_op jit(solution)/shard_map/gather | solution.py:27
  81.3 0.0 copy-start.3
  81.3 11.6 %copy.9 = bf16[896,8,512]{0,2,1:T(8,128)(2,1)} copy(bf16[896,8,512]{2,0,1:T(8,128)(2,1)} %bitcast.37) | data formatting | bytes 14680064 | tf_op jit(solution)/shard_map/transpose | solution.py:10
  92.9 58.4 %all-gather.2.cloned.1.call-done = bf16[1792,4096]{1,0:T(8,128)(2,1)} async-done(((bf16[1792,128]{1,0:T(8,128)(2,1)}), bf16[1792,4096]{1,0:T(8,128)(2,1)}) %all-gather.2.cloned.1.call-update) | async-done | bytes 14680080 | tf_op jit(solution)/shard_map/all_gather | solution.py:31
  151.4 0.0 copy-done.3
  151.4 0.0 copy-start.5
  151.4 0.0 copy-start.4
  151.4 22.7 %fusion = f32[896,64]{0,1:T(8,128)} fusion(bf16[1792,64]{0,1:T(8,128)(2,1)S(1)} %copy-done.3, bf16[896,1792]{1,0:T(8,128)(2,1)} %param.10, bf16[896,4096]{0,1:T(8,128)(2,1)} %bitcast.38, bf16[1792,4096]{1,0:T(8,128)(2,1)} %all-gather.2.cloned.1.call-done), kind=kOutput, calls=%fused_computation.2 | convolution fusion | flops 13363675136 | bytes 25690112 | tf_op jit(solution)/shard_map/dot_general | solution.py:36
  174.1 0.0 all-reduce.3.cloned.1.call-update
  174.1 0.0 reduce-scatter.2.cloned.1.call-start
  174.2 0.0 copy-done.5
  174.2 0.0 copy-done.4
  174.2 0.1 dynamic_slice.6
  174.3 0.1 fusion.8
  174.4 60.4 %all-reduce.3.cloned.1.call-done = (f32[896,64]{0,1:T(8,128)}, f32[896,64]{0,1:T(8,128)}) async-done(((f32[896,64]{0,1:T(8,128)}, f32[896,64]{0,1:T(8,128)}), (f32[896,64]{0,1:T(8,128)}, f32[896,64]{0,1:T(8,128)})) %all-reduce.3.cloned.1.call-update) | async-done | bytes 458768 | tf_op jit(solution)/shard_map/psum | solution.py:40
  234.8 0.8 constant_dynamic-slice_fusion
  235.5 1.3 fusion.1
  236.8 0.1 reshape.161
  236.9 1.0 convolution_convert_fusion
  237.9 0.0 reduce-scatter.2.cloned.1.call-update
  238.0 215.1 %reduce-scatter.2.cloned.1.call-done = bf16[8,512]{1,0:T(8,128)(2,1)} async-done(((bf16[256,512]{1,0:T(8,128)(2,1)}), bf16[8,512]{1,0:T(8,128)(2,1)}) %reduce-scatter.2.cloned.1.call-update) | async-done | bytes 8208 | tf_op jit(solution)/shard_map/reduce_scatter | solution.py:58
  453.1 1.4 reshape.165
  (3 shorter events, 0.0 us)
Async XLA Ops:
  6.5 42.0 %copy-start = (bf16[896,512]{1,0:T(8,128)(2,1)S(1)}, bf16[896,512]{1,0:T(8,128)(2,1)}, u32[]{:S(2)}) copy-start(bf16[896,512]{1,0:T(8,128)(2,1)} %param.8) | copy-start | bytes 2752516
  6.5 61.2 %copy-start.1 = (bf16[896,512]{1,0:T(8,128)(2,1)S(1)}, bf16[896,512]{1,0:T(8,128)(2,1)}, u32[]{:S(2)}) copy-start(bf16[896,512]{1,0:T(8,128)(2,1)} %param.9) | copy-start | bytes 2752516
  6.5 144.8 %all-gather.2.cloned.1.call-start = ((), (), s32[]{:S(2)}) async-start(), calls=%async_computation.1 | async-start | bytes 15138816 | tf_op jit(solution)/shard_map/all_gather | solution.py:31
  7.3 227.5 %all-reduce.3.cloned.1.call-start = ((), (), s32[]{:S(2)}) async-start(), calls=%async_computation.3 | async-start | bytes 917504 | tf_op jit(solution)/shard_map/psum | solution.py:40
  7.3 13.0 %collective-permute-start = (bf16[896,512]{1,0:T(8,128)(2,1)}, bf16[896,512]{1,0:T(8,128)(2,1)S(1)}, u32[]{:S(2)}, u32[]{:S(2)}) collective-permute-start(bf16[896,512]{1,0:T(8,128)(2,1)} %param.9), channel_id=1, source_target_pairs={{0,1},{1,2},{2,3},{3,4},{4,5},{5,6},{6,7},{7,0},{8,9},{9,10},{10,1... | collective-permute-start | bytes 2752520 | tf_op jit(solution)/shard_map/ppermute | solution.py:22
  20.3 12.8 %collective-permute-start.1 = (bf16[896,512]{1,0:T(8,128)(2,1)S(1)}, bf16[896,512]{1,0:T(8,128)(2,1)S(1)}, u32[]{:S(2)}, u32[]{:S(2)}) collective-permute-start(bf16[896,512]{1,0:T(8,128)(2,1)S(1)} %collective-permute-done), channel_id=1, source_target_pairs={{0,1},{1,2},{2,3},{3,4},{4,5},{5,6},{6,7},{7,0},{8,9},{9,10},{10,1... | collective-permute-start | bytes 2752520 | tf_op jit(solution)/shard_map/ppermute | solution.py:22
  20.4 13.7 %collective-permute-start.4 = (bf16[896,512]{1,0:T(8,128)(2,1)}, bf16[896,512]{1,0:T(8,128)(2,1)}, u32[]{:S(2)}, u32[]{:S(2)}) collective-permute-start(bf16[896,512]{1,0:T(8,128)(2,1)} %param.9), channel_id=1, source_target_pairs={{1,0},{2,1},{3,2},{4,3},{5,4},{6,5},{7,6},{0,7},{9,8},{10,9},{11,1... | collective-permute-start | bytes 2752520 | tf_op jit(solution)/shard_map/ppermute | solution.py:24
  33.2 0.9 copy-start.2
  34.1 12.9 %collective-permute-start.2 = (bf16[896,512]{1,0:T(8,128)(2,1)S(1)}, bf16[896,512]{1,0:T(8,128)(2,1)}, u32[]{:S(2)}, u32[]{:S(2)}) collective-permute-start(bf16[896,512]{1,0:T(8,128)(2,1)S(1)} %collective-permute-done.1), channel_id=1, source_target_pairs={{0,1},{1,2},{2,3},{3,4},{4,5},{5,6},{6,7},{7,0},{8,9},{9,10},{10,1... | collective-permute-start | bytes 2752520 | tf_op jit(solution)/shard_map/ppermute | solution.py:22
  34.1 16.4 %collective-permute-start.5 = (bf16[896,512]{1,0:T(8,128)(2,1)}, bf16[896,512]{1,0:T(8,128)(2,1)}, u32[]{:S(2)}, u32[]{:S(2)}) collective-permute-start(bf16[896,512]{1,0:T(8,128)(2,1)} %collective-permute-done.4), channel_id=1, source_target_pairs={{1,0},{2,1},{3,2},{4,3},{5,4},{6,5},{7,6},{0,7},{9,8},{10,9},{11,1... | collective-permute-start | bytes 2752520 | tf_op jit(solution)/shard_map/ppermute | solution.py:24
  47.0 13.1 %collective-permute-start.3 = (bf16[896,512]{1,0:T(8,128)(2,1)}, bf16[896,512]{1,0:T(8,128)(2,1)}, u32[]{:S(2)}, u32[]{:S(2)}) collective-permute-start(bf16[896,512]{1,0:T(8,128)(2,1)} %collective-permute-done.2), channel_id=1, source_target_pairs={{0,1},{1,2},{2,3},{3,4},{4,5},{5,6},{6,7},{7,0},{8,9},{9,10},{10,1... | collective-permute-start | bytes 2752520 | tf_op jit(solution)/shard_map/ppermute | solution.py:22
  50.5 22.6 %collective-permute-start.6 = (bf16[896,512]{1,0:T(8,128)(2,1)}, bf16[896,512]{1,0:T(8,128)(2,1)S(1)}, u32[]{:S(2)}, u32[]{:S(2)}) collective-permute-start(bf16[896,512]{1,0:T(8,128)(2,1)} %collective-permute-done.5), channel_id=1, source_target_pairs={{1,0},{2,1},{3,2},{4,3},{5,4},{6,5},{7,6},{0,7},{9,8},{10,9},{11,1... | collective-permute-start | bytes 2752520 | tf_op jit(solution)/shard_map/ppermute | solution.py:24
  81.3 70.1 %copy-start.3 = (bf16[1792,64]{0,1:T(8,128)(2,1)S(1)}, bf16[1792,64]{0,1:T(8,128)(2,1)}, u32[]{:S(2)}) copy-start(bf16[1792,64]{0,1:T(8,128)(2,1)} %param.13) | copy-start | bytes 688132
  151.4 22.8 %copy-start.5 = (s32[1,8]{1,0:T(1,128)S(1)}, s32[1,8]{1,0:T(1,128)}, u32[]{:S(2)}) copy-start(s32[1,8]{1,0:T(1,128)} %param.14) | copy-start | bytes 100
  151.4 22.9 %copy-start.4 = (s32[256]{0:T(256)S(1)}, s32[256]{0:T(256)}, u32[]{:S(2)}) copy-start(s32[256]{0:T(256)} %param.15) | copy-start | bytes 3076
  174.1 279.0 %reduce-scatter.2.cloned.1.call-start = ((), (), s32[]{:S(2)}) async-start(), calls=%async_computation.2 | async-start | bytes 270336 | tf_op jit(solution)/shard_map/reduce_scatter | solution.py:58
Sparse Core Ops, SparseCore 0:
  9.8 141.4 all-gather.1
  174.3 60.4 all-reduce.2
  239.1 213.9 reduce-scatter.1
